TPU v7x, 1024 devices: a whole 8x8x8 slice. The times are simulated.
1024 devices in a mesh: ctx: 16 (over x_hi, y), dp: 64 (over z, x_lo, core).
Axes of the slice: x: 8 (x_hi: 2, x_lo: 4; x = x_hi * 4 + x_lo), y: 8, z: 8, core: 2. Of those that a mesh axis runs over, the one named last changes fastest.
Arguments:
- queries: bfloat16 [64, 2048, 1024], P('dp', 'ctx'), may hold values from -6 to 6
- keys_in: bfloat16 [64, 2048, 256], P('dp', 'ctx'), may hold values from -6 to 6
- values_in: bfloat16 [64, 2048, 256], P('dp', 'ctx'), may hold values from -6 to 6
- patch_order: int32 [64, 16, 128], P('dp', 'ctx'), may hold values from 0 to 127, each once within a row
- block_mask: int32 [64, 64, 8], P('dp', 'ctx'), may hold values 0 or 1
- out_weight: bfloat16 [1024, 1024], P('dp'), may hold values from -0.1875 to 0.1875
- cotangent: bfloat16 [64, 2048, 1024], P('dp', 'ctx'), may hold values from -6 to 6
Outputs:
- mixed: bfloat16 [64, 2048, 1024], P('dp', 'ctx')
- grad_queries: bfloat16 [64, 2048, 1024], P('dp', 'ctx')
- grad_keys: bfloat16 [64, 2048, 256], P('dp', 'ctx')
- grad_values: bfloat16 [64, 2048, 256], P('dp', 'ctx')
- grad_weight: float32 [1024, 1024], P('dp', 'ctx')
Inputs may be any that keep to these rules, and one draw needn't show every extreme that they name: `patch_order`: each row of 128 entries is a permutation.
All inputs are finite; a program needn't handle non-finite values. No bound on the sum of `block_mask` on one device may be relied on, other than what follows from the above.
Results may differ from a plain program's by a relative error of at most 0.015.
Values may be sent and summed in bfloat16 or wider, within the bound.
A program may use at most 32 MiB of HBM per device.

v0:
```python
import math

import jax
import jax.numpy as jnp
from jax import lax
from jax.sharding import PartitionSpec as P

QUERY_HEADS = 8
KEY_VALUE_HEADS = 2
HEAD_WIDTH = 128
BLK = 32


def with_halo(block, sides, width):
    for axis, dim in sides:
        count = lax.axis_size(axis)
        forward = [(i, i + 1) for i in range(count - 1)]
        forward.append((count - 1, 0))
        backward = [(target, source) for source, target in forward]
        low = lax.ppermute(
            lax.slice_in_dim(block, block.shape[dim] - width, None, axis=dim), axis, forward
        )
        high = lax.ppermute(lax.slice_in_dim(block, 0, width, axis=dim), axis, backward)
        block = jnp.concatenate([low, block, high], axis=dim)
    return block


def shards(queries, keys_in, values_in, patch_order, block_mask, out_weight, cotangent):
    scale = 1.0 / math.sqrt(HEAD_WIDTH)
    query_group = QUERY_HEADS // KEY_VALUE_HEADS
    token_rows = queries.shape[1]
    key_head_width = keys_in.shape[2]
    row_position = patch_order[0, 0]
    query_sequence = jnp.take(queries[0], row_position, axis=0)
    key_sequence = jnp.take(keys_in[0], row_position, axis=0)
    value_sequence = jnp.take(values_in[0], row_position, axis=0)
    dy_seq = jnp.take(cotangent[0], row_position, axis=0)
    kv_pair = jnp.concatenate([key_sequence, value_sequence], axis=1)
    neighbour_band = with_halo(kv_pair, (("ctx", 0),), token_rows)
    key_band = neighbour_band[:, :key_head_width].reshape(
        3 * token_rows, KEY_VALUE_HEADS, HEAD_WIDTH
    )
    value_band = neighbour_band[:, key_head_width:].reshape(
        3 * token_rows, KEY_VALUE_HEADS, HEAD_WIDTH
    )
    weight_all = lax.all_gather(out_weight, "dp", axis=0, tiled=True)
    expanded = jnp.repeat(jnp.repeat(block_mask[0], BLK, 0), BLK, 1) > 0
    allowed = jnp.concatenate(
        [
            expanded[:, :token_rows],
            jnp.ones((token_rows, token_rows), bool),
            expanded[:, token_rows:],
        ],
        1,
    )
    allowed = allowed[None, None]
    query_four = query_sequence.reshape(token_rows, KEY_VALUE_HEADS, query_group, HEAD_WIDTH)
    scores = (
        jnp.einsum("tkgd,skd->kgts", query_four, key_band, preferred_element_type=jnp.float32)
        * scale
    )
    scores = jnp.where(allowed, scores, -1e30)
    highest = jnp.max(scores, axis=-1, keepdims=True)
    weights = jnp.where(allowed, jnp.exp(scores - highest), 0.0)
    probs = weights / jnp.sum(weights, axis=-1, keepdims=True)
    probs_b = probs.astype(jnp.bfloat16)
    attended_f = jnp.einsum(
        "kgts,skd->tkgd", probs_b, value_band, preferred_element_type=jnp.float32
    )
    attended = attended_f.astype(jnp.bfloat16).reshape(token_rows, query_sequence.shape[1])
    mixed_seq = jnp.dot(attended, weight_all, preferred_element_type=jnp.float32).astype(
        jnp.bfloat16
    )
    mixed_out = jnp.zeros_like(mixed_seq).at[row_position].set(mixed_seq)
    attention_gradient = lax.dot_general(
        dy_seq, weight_all, (((1,), (1,)), ((), ())), preferred_element_type=jnp.float32
    ).astype(jnp.bfloat16)
    attention_gradient4 = attention_gradient.reshape(
        token_rows, KEY_VALUE_HEADS, query_group, HEAD_WIDTH
    )
    d_probs = jnp.einsum(
        "tkgd,skd->kgts", attention_gradient4, value_band, preferred_element_type=jnp.float32
    )
    delta = jnp.sum(attention_gradient4.astype(jnp.float32) * attended_f, axis=-1)
    delta = jnp.transpose(delta, (1, 2, 0))[..., None]
    d_scores_b = (probs * (d_probs - delta)).astype(jnp.bfloat16)
    grad_q_seq = (
        jnp.einsum("kgts,skd->tkgd", d_scores_b, key_band, preferred_element_type=jnp.float32)
        * scale
    ).astype(jnp.bfloat16)
    grad_q_out = (
        jnp.zeros_like(query_sequence)
        .at[row_position]
        .set(grad_q_seq.reshape(token_rows, query_sequence.shape[1]))
    )
    part_k = (
        jnp.einsum("kgts,tkgd->skd", d_scores_b, query_four, preferred_element_type=jnp.float32)
        * scale
    ).astype(jnp.bfloat16)
    part_v = jnp.einsum(
        "kgts,tkgd->skd", probs_b, attention_gradient4, preferred_element_type=jnp.float32
    ).astype(jnp.bfloat16)
    part_both = jnp.concatenate(
        [
            part_k.reshape(3 * token_rows, key_head_width),
            part_v.reshape(3 * token_rows, key_head_width),
        ],
        axis=1,
    )
    outgoing = jnp.concatenate([part_both[:token_rows], part_both[2 * token_rows :]], axis=0)
    arrived = with_halo(outgoing, (("ctx", 0),), token_rows)
    summed = (
        part_both[token_rows : 2 * token_rows].astype(jnp.float32)
        + arrived[:token_rows].astype(jnp.float32)
        + arrived[3 * token_rows :].astype(jnp.float32)
    )
    summed = summed.astype(jnp.bfloat16)
    grad_k_out = jnp.zeros_like(key_sequence).at[row_position].set(summed[:, :key_head_width])
    grad_v_out = jnp.zeros_like(value_sequence).at[row_position].set(summed[:, key_head_width:])
    total_tokens = lax.axis_size("dp") * token_rows * lax.axis_size("ctx")
    norm_factor = 1.0 / math.sqrt(total_tokens)
    data_rows = lax.psum_scatter(
        lax.dot_general(
            attended, dy_seq, (((0,), (0,)), ((), ())), preferred_element_type=jnp.float32
        ),
        "dp",
        scatter_dimension=0,
        tiled=True,
    )
    grad_weight = (
        lax.psum_scatter(
            data_rows.astype(jnp.bfloat16), "ctx", scatter_dimension=1, tiled=True
        ).astype(jnp.float32)
        * norm_factor
    )
    return (mixed_out[None], grad_q_out[None], grad_k_out[None], grad_v_out[None], grad_weight)


def solution(mesh):
    in_specs = (
        P("dp", "ctx", None),
        P("dp", "ctx", None),
        P("dp", "ctx", None),
        P("dp", "ctx", None),
        P("dp", "ctx", None),
        P("dp", None),
        P("dp", "ctx", None),
    )
    out_specs = (
        P("dp", "ctx", None),
        P("dp", "ctx", None),
        P("dp", "ctx", None),
        P("dp", "ctx", None),
        P("dp", "ctx"),
    )
    return jax.shard_map(shards, mesh=mesh, in_specs=in_specs, out_specs=out_specs, check_vma=False)
```

profile of v0, /device:TPU:1, one launch (start us, length us, event | category | flops | bytes accessed | tf_op | source)
XLA Modules:
  0.0 664.7 jit_solution(13715630225452615563)
XLA Ops:
  8.6 1.6 gather_fusion.1
  10.2 1.6 gather_fusion
  12.7 11.6 %collective-permute-start.1 = (bf16[128,512]{1,0:T(8,128)(2,1)S(1)}, bf16[128,512]{1,0:T(8,128)(2,1)S(1)}, u32[]{:S(2)}, u32[]{:S(2)}) collective-permute-start(bf16[128,512]{1,0:T(8,128)(2,1)S(1)} %pad_maximum_fusion.2), channel_id=1, source_target_pairs={{64,0},{128,64},{192,128},{256,192},{320,256},{384,320},{448,384},... | collective-permute-start | bytes 393224 | tf_op jit(solution)/shard_map/ppermute | solution.py:23
  24.3 1.9 collective-permute-start
  26.6 0.9 gather_fusion.3
  27.4 0.9 gather_fusion.2
  28.8 7.4 %collective-permute-done = bf16[128,512]{1,0:T(8,128)(2,1)S(1)} collective-permute-done((bf16[128,512]{1,0:T(8,128)(2,1)S(1)}, bf16[128,512]{1,0:T(8,128)(2,1)S(1)}, u32[]{:S(2)}, u32[]{:S(2)}) %collective-permute-start) | collective-permute-done | bytes 131104 | tf_op jit(solution)/shard_map/ppermute | solution.py:20
  36.4 0.8 copy.43
  37.2 0.8 fusion.30
  38.2 105.7 %all-gather.2.cloned.1.call-done = bf16[1024,1024]{1,0:T(8,128)(2,1)} async-done(((bf16[16,1024]{1,0:T(8,128)(2,1)}), bf16[1024,1024]{1,0:T(8,128)(2,1)}) %all-gather.2.cloned.1.call-update) | async-done | bytes 2097168 | tf_op jit(solution)/shard_map/all_gather | solution.py:46
  143.9 2.4 convolution_convert_fusion
  146.5 1.3 multiply_reduce_fusion
  147.8 2.7 fusion.15
  151.2 1.4 fusion.3
  152.6 0.9 copy-done.3
  153.5 1.1 fusion.6
  154.6 1.9 copy.57
  156.5 2.0 fusion.7
  158.5 1.7 copy.58
  160.2 1.7 fusion.9
  161.9 3.1 collective-permute-start.2
  165.1 8.6 %collective-permute-start.3 = (bf16[128,512]{1,0:T(8,128)(2,1)S(1)}, bf16[128,512]{1,0:T(8,128)(2,1)}, u32[]{:S(2)}, u32[]{:S(2)}) collective-permute-start(bf16[128,512]{1,0:T(8,128)(2,1)S(1)} %get-tuple-element.10), channel_id=1, source_target_pairs={{64,0},{128,64},{192,128},{256,192},{320,256},{384,320},{448,384},... | collective-permute-start | bytes 393224 | tf_op jit(solution)/shard_map/ppermute | solution.py:23
  173.6 1.2 convolution_convert_fusion.1
  175.3 2.2 scatter_custom_fusion
  177.5 1.8 scatter_custom_fusion.1
  179.3 258.7 %reduce-scatter.5.cloned.1.call-done = f32[16,1024]{1,0:T(8,128)} async-done(((f32[1024,1024]{1,0:T(8,128)}), f32[16,1024]{1,0:T(8,128)}) %reduce-scatter.5.cloned.1.call-update) | async-done | bytes 65552 | tf_op jit(solution)/shard_map/reduce_scatter | solution.py:122
  438.0 0.8 convert_element_type.70
  438.9 0.9 copy.74
  439.8 1.0 add_convert_fusion
  440.8 1.6 scatter_custom_fusion.3
  442.4 1.6 scatter_custom_fusion.2
  444.0 212.8 %reduce-scatter.7.cloned.1.call-done = bf16[64,16]{1,0:T(8,128)(2,1)} async-done(((bf16[1024,16]{1,0:T(8,128)(2,1)}), bf16[64,16]{1,0:T(8,128)(2,1)}) %reduce-scatter.7.cloned.1.call-update) | async-done | bytes 2064
  (62 shorter events, 6.0 us)
Async XLA Ops:
  7.2 19.4 %copy-start = (bf16[1,128,1024]{2,1,0:T(8,128)(2,1)S(1)}, bf16[1,128,1024]{2,1,0:T(8,128)(2,1)}, u32[]{:S(2)}) copy-start(bf16[1,128,1024]{2,1,0:T(8,128)(2,1)} %param.17) | copy-start | bytes 786436
  7.2 19.1 %copy-start.12 = (s32[1,4,8]{2,1,0:T(4,128)S(1)}, s32[1,4,8]{2,1,0:T(4,128)}, u32[]{:S(2)}) copy-start(s32[1,4,8]{2,1,0:T(4,128)} %param.15) | copy-start | bytes 388
  7.2 136.7 %all-gather.2.cloned.1.call-start = ((), (), s32[]{:S(2)}) async-start(), calls=%async_computation.2 | async-start | bytes 2129920 | tf_op jit(solution)/shard_map/all_gather | solution.py:46
  7.9 430.1 %reduce-scatter.5.cloned.1.call-start = ((), (), s32[]{:S(2)}) async-start(), calls=%async_computation.3 | async-start | bytes 4259840 | tf_op jit(solution)/shard_map/reduce_scatter | solution.py:122
  11.9 15.6 %copy-start.1 = (bf16[1,128,1024]{2,1,0:T(8,128)(2,1)S(1)}, bf16[1,128,1024]{2,1,0:T(8,128)(2,1)}, u32[]{:S(2)}) copy-start(bf16[1,128,1024]{2,1,0:T(8,128)(2,1)} %param.11) | copy-start | bytes 786436
  12.7 16.1 %collective-permute-start.1 = (bf16[128,512]{1,0:T(8,128)(2,1)S(1)}, bf16[128,512]{1,0:T(8,128)(2,1)S(1)}, u32[]{:S(2)}, u32[]{:S(2)}) collective-permute-start(bf16[128,512]{1,0:T(8,128)(2,1)S(1)} %pad_maximum_fusion.2), channel_id=1, source_target_pairs={{64,0},{128,64},{192,128},{256,192},{320,256},{384,320},{448,384},... | collective-permute-start | bytes 393224 | tf_op jit(solution)/shard_map/ppermute | solution.py:23
  24.3 11.8 %collective-permute-start = (bf16[128,512]{1,0:T(8,128)(2,1)S(1)}, bf16[128,512]{1,0:T(8,128)(2,1)S(1)}, u32[]{:S(2)}, u32[]{:S(2)}) collective-permute-start(bf16[128,512]{1,0:T(8,128)(2,1)S(1)} %pad_maximum_fusion.2), channel_id=1, source_target_pairs={{0,64},{64,128},{128,192},{192,256},{256,320},{320,384},{384,448},... | collective-permute-start | bytes 393224 | tf_op jit(solution)/shard_map/ppermute | solution.py:20
  28.6 9.5 %copy-start.8 = (bf16[128,1024]{0,1:T(8,128)(2,1)}, bf16[128,1024]{0,1:T(8,128)(2,1)S(1)}, u32[]{:S(2)}) copy-start(bf16[128,1024]{0,1:T(8,128)(2,1)S(1)} %copy.76) | copy-start | bytes 786436
  36.4 1.6 copy-start.10
  146.5 4.7 copy-start.5
  150.6 0.7 copy-start.13
  150.6 506.2 %reduce-scatter.7.cloned.1.call-start = ((), (), s32[]{:S(2)}) async-start(), calls=%async_computation.4 | async-start | bytes 278528
  151.2 2.3 copy-start.9
  152.6 0.9 copy-start.3
  154.6 19.0 %copy-start.2 = (bf16[1024,1024]{1,0:T(8,128)(2,1)S(1)}, bf16[1024,1024]{1,0:T(8,128)(2,1)}, u32[]{:S(2)}) copy-start(bf16[1024,1024]{1,0:T(8,128)(2,1)} %all-gather.2.cloned.1.call-done) | copy-start | bytes 6291460
  160.2 14.6 %copy-start.4 = (bf16[2,4,128,384]{2,3,1,0:T(8,128)(2,1)S(1)}, bf16[2,4,128,384]{2,3,1,0:T(8,128)(2,1)}, u32[]{:S(2)}) copy-start(bf16[2,4,128,384]{2,3,1,0:T(8,128)(2,1)} %copy-done.3) | copy-start | bytes 2359300
  160.2 14.6 %copy-start.11 = (bf16[384,256]{0,1:T(8,128)(2,1)S(1)}, bf16[384,256]{0,1:T(8,128)(2,1)}, u32[]{:S(2)}) copy-start(bf16[384,256]{0,1:T(8,128)(2,1)} %copy-done.10) | copy-start | bytes 589828
  161.9 277.8 %collective-permute-start.2 = (bf16[128,512]{1,0:T(8,128)(2,1)}, bf16[128,512]{1,0:T(8,128)(2,1)}, u32[]{:S(2)}, u32[]{:S(2)}) collective-permute-start(bf16[128,512]{1,0:T(8,128)(2,1)} %get-tuple-element.9), channel_id=1, source_target_pairs={{0,64},{64,128},{128,192},{192,256},{256,320},{320,384},{384,448},... | collective-permute-start | bytes 393224 | tf_op jit(solution)/shard_map/ppermute | solution.py:20
  165.1 274.7 %collective-permute-start.3 = (bf16[128,512]{1,0:T(8,128)(2,1)S(1)}, bf16[128,512]{1,0:T(8,128)(2,1)}, u32[]{:S(2)}, u32[]{:S(2)}) collective-permute-start(bf16[128,512]{1,0:T(8,128)(2,1)S(1)} %get-tuple-element.10), channel_id=1, source_target_pairs={{64,0},{128,64},{192,128},{256,192},{320,256},{384,320},{448,384},... | collective-permute-start | bytes 393224 | tf_op jit(solution)/shard_map/ppermute | solution.py:23
  174.8 264.9 %copy-start.6 = (bf16[384,256]{1,0:T(8,128)(2,1)S(1)}, bf16[384,256]{1,0:T(8,128)(2,1)}, u32[]{:S(2)}) copy-start(bf16[384,256]{1,0:T(8,128)(2,1)} %copy.57) | copy-start | bytes 589828
  174.8 264.9 %copy-start.7 = (bf16[384,256]{1,0:T(8,128)(2,1)S(1)}, bf16[384,256]{1,0:T(8,128)(2,1)}, u32[]{:S(2)}) copy-start(bf16[384,256]{1,0:T(8,128)(2,1)} %copy.58) | copy-start | bytes 589828
Sparse Core Ops, SparseCore 0:
  10.8 133.0 all-gather.1
  150.7 287.2 reduce-scatter.4
  444.5 212.3 reduce-scatter.6
where the time goes:
time: 669 us; the launch traced here: 665 us
  waiting for transfers between devices  585 us (87%)
  starting transfers between devices  25.4 us (4%)
  local copies, waits for them, and re-layouts  20.8 us (3%)
  between operations  14.1 us (2%)
  matrix products  13.2 us (2%)
    reduce_scatter x1, waiting for transfers between devices, shards(): lax.psum_scatter(lax.dot_general(attended, dy_seq, (((0,), (0,)), ((), ()...  259 us
    unnamed x4, waiting for transfers between devices  214 us
    all_gather x1, waiting for transfers between devices, shards(): weight_all = lax.all_gather(out_weight, 'dp', axis=0, tiled=True)  106 us
    ppermute x2, starting transfers between devices, with_halo(): lax.ppermute(lax.slice_in_dim(block, 0, width, axis=dim), axis, backward)  20.2 us
  transfers between devices with their start and end apart: 7, of which 4 were waited for; matrix products, arithmetic and copies ran while one was open for 5% of the time, Pallas kernels for 0%

commit v1 on v0

v1 whole, which is shorter than its diff:
```python
import functools
import math

import jax
import jax.numpy as jnp
from jax import lax
from jax.experimental import pallas as pl
from jax.experimental.pallas import tpu as pltpu
from jax.sharding import PartitionSpec as P

MESH = pl.DeviceIdType.MESH
BF = jnp.bfloat16
F32 = jnp.float32
HD = 128
T = 128
D = 1024
GROUP = 4
GROUPS = 2
KV = 256
BLK = 32
D7 = (1, -1, 2, -2, 3, -3, 4)
NT = (((1,), (1,)), ((), ()))
NN = (((1,), (0,)), ((), ()))


def kernel(
    mask_s, order_v, q_h, k_h, v_h, w_h, dy_h,
    mixed_o, gq_o, gk_o, gv_o, gw_o,
    q_v, dy2, kb, vb, order_n, w_full,
    qst, dast, ktr, vtr, st, pf, pb, dsb, att_t, lhs, att,
    part_k, part_v, got_k, got_v,
    ga, gb, ra1, rb1, ga2, gb2, ra2, rb2, gy, ry,
    loc_sem, halo_ss, halo_rs, wz_ss, wz_rs, wx_ss, wx_rs, wc_ss, wc_rs,
    core_ss, core_rs, ph_ss, ph_rs,
    a1_ss, a1_rs, b1_ss, b1_rs, a2_ss, a2_rs, b2_ss, b2_rs, y_ss, y_rs,
):
    c = lax.axis_index("ctx")
    d = lax.axis_index("dp")
    xh, y = c // 8, c % 8
    z, xl, k = d // 8, (d // 2) % 4, d % 2
    x = xh * 4 + xl

    def dev(x_, y_, z_, k_):
        return ((x_ // 4) * 8 + y_, z_ * 8 + (x_ % 4) * 2 + k_)

    def zdev(s):
        return dev(x, y, (z + s + 8) % 8, k)

    def xdev(s):
        return dev((x + s + 8) % 8, y, z, k)

    def ydev(s):
        return dev(x, (y + s + 8) % 8, z, k)

    def cdev(s):
        return ((c + s + 16) % 16, d)

    other = 1 - k
    mate = dev(x, y, z, other)

    def rcopy(src, dst, ss, rs, to):
        return pltpu.make_async_remote_copy(
            src_ref=src, dst_ref=dst, send_sem=ss, recv_sem=rs, device_id=to, device_id_type=MESH
        )

    loc = [
        pltpu.make_async_copy(q_h, q_v, loc_sem.at[0]),
        pltpu.make_async_copy(k_h, kb.at[1], loc_sem.at[1]),
        pltpu.make_async_copy(v_h, vb.at[1], loc_sem.at[2]),
        pltpu.make_async_copy(dy_h, dy2.at[0], loc_sem.at[3]),
        pltpu.make_async_copy(w_h, w_full.at[z, xl, k], loc_sem.at[4]),
    ]
    for cp in loc:
        cp.start()

    bar = pltpu.get_barrier_semaphore()
    friends = [cdev(1), cdev(-1), mate]
    for s in D7:
        friends += [zdev(s), xdev(s), ydev(s)]
    for f in friends:
        pl.semaphore_signal(bar, inc=1, device_id=f, device_id_type=MESH)
    pl.semaphore_wait(bar, len(friends))

    sends = []

    def go(cp):
        cp.start()
        sends.append(cp)
        return cp

    halo = []
    for i, (s, slot) in enumerate(((1, 0), (-1, 2))):
        halo.append(go(rcopy(k_h, kb.at[slot], halo_ss.at[3 * i], halo_rs.at[3 * i], cdev(s))))
        halo.append(go(rcopy(v_h, vb.at[slot], halo_ss.at[3 * i + 1], halo_rs.at[3 * i + 1], cdev(s))))
        halo.append(go(rcopy(order_v, order_n.at[i], halo_ss.at[3 * i + 2], halo_rs.at[3 * i + 2], cdev(s))))
    for i, s in enumerate(D7):
        go(rcopy(w_h, w_full.at[z, xl, k], wz_ss.at[i], wz_rs.at[i], zdev(s)))
    dy_c = go(rcopy(dy_h, dy2.at[1], core_ss.at[0], core_rs.at[0], mate))

    for cp in loc[:3]:
        cp.wait()
    for h in range(8):
        qst[h * T : (h + 1) * T, :] = q_v[:, h * HD : (h + 1) * HD]
    for g in range(GROUPS):
        st[g, T : 2 * T, :] = lax.dot_general(
            kb[1, :, g * HD : (g + 1) * HD], qst[g * 512 : (g + 1) * 512, :], NT,
            preferred_element_type=F32,
        )
    jcol = lax.broadcasted_iota(jnp.int32, (T, T), 1)
    irow = lax.broadcasted_iota(jnp.int32, (T, T), 0)
    jblk = jcol // BLK

    def key_block(order):
        hit = irow == jnp.broadcast_to(order, (T, T))
        return jnp.sum(jnp.where(hit, jblk, 0).astype(F32), axis=1, keepdims=True)

    own_hit = (irow == jnp.broadcast_to(order_v[...], (T, T))).astype(F32).astype(BF)
    jrow = (lax.broadcasted_iota(jnp.int32, (8, T), 1) // BLK).astype(F32).astype(BF)
    q_block = lax.dot_general(jrow, own_hit, NT, preferred_element_type=F32)[0:1]

    loc[4].wait()
    for i, s in enumerate(D7):
        there = w_full.at[(z - s + 8) % 8, xl, k]
        rcopy(w_h, there, wz_ss.at[i], wz_rs.at[i], zdev(s)).wait_recv()
    column = w_full.at[:, xl, k]
    go(rcopy(column, column, wx_ss.at[0], wx_rs.at[0], xdev(1)))
    go(rcopy(column, column, wx_ss.at[1], wx_rs.at[1], xdev(-1)))
    for i, s in ((2, 2), (3, -2)):
        part = w_full.at[pl.ds((i - 2) * 4, 4), xl, k]
        go(rcopy(part, part, wx_ss.at[i], wx_rs.at[i], xdev(s)))
    go(rcopy(column, column, wc_ss.at[0], wc_rs.at[0], mate))

    for cp in halo:
        cp.wait_recv()
    for i, slot in ((0, 0), (1, 2)):
        kblk = key_block(order_n[i])
        allow = jnp.zeros((T, T), F32)
        for b2 in range(4):
            row = jnp.zeros((1, T), F32)
            for b1 in range(4):
                seen = jnp.full((1, T), mask_s[b1, 4 * i + b2], jnp.int32).astype(F32)
                row = row + jnp.where(q_block == float(b1), seen, 0.0)
            allow = allow + jnp.where(kblk == float(b2), jnp.broadcast_to(row, (T, T)), 0.0)
        allow4 = jnp.concatenate([allow] * GROUP, axis=1)
        for g in range(GROUPS):
            s_g = lax.dot_general(
                kb[slot, :, g * HD : (g + 1) * HD], qst[g * 512 : (g + 1) * 512, :], NT,
                preferred_element_type=F32,
            )
            st[g, slot * T : (slot + 1) * T, :] = jnp.where(allow4 > 0.5, s_g, -1e30)
    scale = 1.0 / math.sqrt(HD)
    to_two = scale * math.log2(math.e)
    for g in range(GROUPS):
        top = jnp.max(st[g], axis=0, keepdims=True)
        e = jnp.exp2((st[g] - top) * to_two)
        p = e * (1.0 / jnp.sum(e, axis=0, keepdims=True))
        pf[g] = p
        pb[g] = p.astype(BF)
        v_g = vb[:, :, g * HD : (g + 1) * HD].reshape(3 * T, HD)
        vtr[g] = v_g.T
        at = jnp.dot(vtr[g], pb[g], preferred_element_type=F32).astype(BF)
        for j in range(GROUP):
            h = g * GROUP + j
            att_t[h * 4 : (h + 1) * 4] = at[:, j * T : (j + 1) * T].reshape(4, 2, 16, T)
            att[:, h * HD : (h + 1) * HD] = at[:, j * T : (j + 1) * T].T
    a_c = go(rcopy(att_t.at[:, other], lhs.at[1], core_ss.at[1], core_rs.at[1], mate))
    for g in range(GROUPS):
        ktr[g] = kb[:, :, g * HD : (g + 1) * HD].reshape(3 * T, HD).T

    loc[3].wait()
    dy_c.wait_recv()
    lhs[0] = att_t[:, k]
    a_c.wait_recv()
    left = jnp.concatenate([lhs[0].reshape(512, T), lhs[1].reshape(512, T)], axis=1)
    right = dy2[...].reshape(2 * T, D)
    for xh_ in range(2):
        g_a = jnp.dot(left, right[:, xh_ * 512 : xh_ * 512 + 256], preferred_element_type=F32)
        ga[:, :, :, xh_ * 256 : (xh_ + 1) * 256] = g_a.astype(BF).reshape(8, 4, 16, 256)
    a1 = []
    for i, s in enumerate(D7):
        a1.append(go(rcopy(ga.at[(z + s + 8) % 8], ra1.at[i], a1_ss.at[i], a1_rs.at[i], zdev(s))))
    for xh_ in range(2):
        g_b = jnp.dot(left, right[:, xh_ * 512 + 256 : xh_ * 512 + 512], preferred_element_type=F32)
        g_b = g_b.astype(BF).reshape(8, 4, 16, 256)
        for xl_ in range(4):
            gb[xh_ * 4 + xl_] = g_b[:, xl_]
    b1 = []
    for i, s in enumerate(D7):
        b1.append(go(rcopy(gb.at[(x + s + 8) % 8], rb1.at[i], b1_ss.at[i], b1_rs.at[i], xdev(s))))

    for i, s in ((0, 1), (1, -1)):
        there = w_full.at[:, (xl - s + 4) % 4, k]
        rcopy(there, there, wx_ss.at[i], wx_rs.at[i], xdev(s)).wait_recv()
        go(rcopy(there, there, wc_ss.at[i + 1], wc_rs.at[i + 1], mate))
    for i, s in ((2, 2), (3, -2)):
        there = w_full.at[pl.ds((i - 2) * 4, 4), (xl + 2) % 4, k]
        rcopy(there, there, wx_ss.at[i], wx_rs.at[i], xdev(s)).wait_recv()
    there = w_full.at[:, (xl + 2) % 4, k]
    go(rcopy(there, there, wc_ss.at[3], wc_rs.at[3], mate))
    for i, s in ((0, 0), (1, -1), (2, 1), (3, 2)):
        there = w_full.at[:, (xl + s + 4) % 4, other]
        rcopy(there, there, wc_ss.at[i], wc_rs.at[i], mate).wait_recv()

    for h in range(8):
        dast[h * T : (h + 1) * T, :] = lax.dot_general(
            dy2[0], w_full[h].reshape(HD, D), NT, preferred_element_type=F32
        ).astype(BF)
    part = []
    for g in range(GROUPS):
        pv = jnp.dot(pb[g], dast[g * 512 : (g + 1) * 512, :], preferred_element_type=F32)
        part_v[:, :, g * HD : (g + 1) * HD] = pv.astype(BF).reshape(3, T, HD)
    part.append(go(rcopy(part_v.at[0], got_v.at[0], ph_ss.at[0], ph_rs.at[0], cdev(-1))))
    part.append(go(rcopy(part_v.at[2], got_v.at[1], ph_ss.at[1], ph_rs.at[1], cdev(1))))
    for g in range(GROUPS):
        v_g = vb[:, :, g * HD : (g + 1) * HD].reshape(3 * T, HD)
        dp_ = lax.dot_general(
            v_g, dast[g * 512 : (g + 1) * 512, :], NT, preferred_element_type=F32
        )
        delta = jnp.sum(pb[g].astype(F32) * dp_, axis=0, keepdims=True)
        dsb[g] = (pf[g] * (dp_ - delta)).astype(BF)
        pk = jnp.dot(dsb[g], qst[g * 512 : (g + 1) * 512, :], preferred_element_type=F32)
        part_k[:, :, g * HD : (g + 1) * HD] = (pk * scale).astype(BF).reshape(3, T, HD)
    part.append(go(rcopy(part_k.at[0], got_k.at[0], ph_ss.at[2], ph_rs.at[2], cdev(-1))))
    part.append(go(rcopy(part_k.at[2], got_k.at[1], ph_ss.at[3], ph_rs.at[3], cdev(1))))

    for cp in a1:
        cp.wait_recv()
    s_a = ga[z].astype(F32)
    for i in range(7):
        s_a = s_a + ra1[i].astype(F32)
    s_a = s_a.astype(BF)
    for xh_ in range(2):
        ga2[xh_ * 4 : (xh_ + 1) * 4] = s_a[:, :, xh_ * 256 : (xh_ + 1) * 256]
    a2 = []
    for i, s in enumerate(D7):
        a2.append(go(rcopy(ga2.at[(x + s + 8) % 8], ra2.at[i], a2_ss.at[i], a2_rs.at[i], xdev(s))))
    for cp in b1:
        cp.wait_recv()
    s_b = gb[x].astype(F32)
    for i in range(7):
        s_b = s_b + rb1[i].astype(F32)
    gb2[...] = s_b.astype(BF)
    b2 = []
    for i, s in enumerate(D7):
        b2.append(go(rcopy(gb2.at[(z + s + 8) % 8], rb2.at[i], b2_ss.at[i], b2_rs.at[i], zdev(s))))

    mixed_o[...] = jnp.dot(
        att[...], w_full[...].reshape(D, D), preferred_element_type=F32
    ).astype(BF)
    for g in range(GROUPS):
        gq = jnp.dot(ktr[g], dsb[g], preferred_element_type=F32) * scale
        for j in range(GROUP):
            h = g * GROUP + j
            gq_o[:, h * HD : (h + 1) * HD] = gq[:, j * T : (j + 1) * T].astype(BF).T

    for cp in a2:
        cp.wait_recv()
    f_a = ga2[x].astype(F32)
    for i in range(7):
        f_a = f_a + ra2[i].astype(F32)
    gy[0] = f_a[:, :128]
    gy[1] = f_a[:, 128:]
    for cp in b2:
        cp.wait_recv()
    f_b = gb2[z].astype(F32)
    for i in range(7):
        f_b = f_b + rb2[i].astype(F32)
    gy[2] = f_b[:, :128]
    gy[3] = f_b[:, 128:]
    legs = []
    for i, s in enumerate(D7):
        to = (y + s + 8) % 8
        legs.append(go(rcopy(gy.at[to // 2], ry.at[i], y_ss.at[i], y_rs.at[i], ydev(s))))

    for cp in part:
        cp.wait_recv()
    gv_o[...] = (part_v[1].astype(F32) + got_v[0].astype(F32) + got_v[1].astype(F32)).astype(BF)
    gk_o[...] = (part_k[1].astype(F32) + got_k[0].astype(F32) + got_k[1].astype(F32)).astype(BF)

    for cp in legs:
        cp.wait_recv()
    total = gy[y // 2]
    for i in range(7):
        total = total + ry[i]
    norm = 1.0 / math.sqrt(64 * 16 * T)
    odd = jnp.full((16, 64), y % 2, jnp.int32) > 0
    gw_o[...] = jnp.where(odd, total[:, 64:], total[:, :64]) * norm

    for cp in sends:
        cp.wait_send()


def shards(queries, keys_in, values_in, patch_order, block_mask, out_weight, cotangent):
    dma = pltpu.SemaphoreType.DMA
    vm = pltpu.VMEM
    any_ = pl.BlockSpec(memory_space=pl.ANY)
    in_vmem = pl.BlockSpec(memory_space=pltpu.VMEM)
    scratch = [
        vm((T, D), BF),
        vm((2, T, D), BF),
        vm((3, T, KV), BF),
        vm((3, T, KV), BF),
        vm((2, 1, T), jnp.int32),
        vm((8, 4, 2, 16, D), BF),
        vm((8 * T, HD), BF),
        vm((8 * T, HD), BF),
        vm((GROUPS, HD, 3 * T), BF),
        vm((GROUPS, HD, 3 * T), BF),
        vm((GROUPS, 3 * T, 512), F32),
        vm((GROUPS, 3 * T, 512), F32),
        vm((GROUPS, 3 * T, 512), BF),
        vm((GROUPS, 3 * T, 512), BF),
        vm((32, 2, 16, T), BF),
        vm((2, 32, 16, T), BF),
        vm((T, D), BF),
        vm((3, T, KV), BF),
        vm((3, T, KV), BF),
        vm((2, T, KV), BF),
        vm((2, T, KV), BF),
        vm((8, 4, 16, 512), BF),
        vm((8, 8, 16, 256), BF),
        vm((7, 4, 16, 512), BF),
        vm((7, 8, 16, 256), BF),
        vm((8, 16, 256), BF),
        vm((8, 16, 256), BF),
        vm((7, 16, 256), BF),
        vm((7, 16, 256), BF),
        vm((4, 16, 128), F32),
        vm((7, 16, 128), F32),
        dma((5,)),
        dma((6,)), dma((6,)),
        dma((7,)), dma((7,)),
        dma((4,)), dma((4,)),
        dma((4,)), dma((4,)),
        dma((2,)), dma((2,)),
        dma((4,)), dma((4,)),
        dma((7,)), dma((7,)),
        dma((7,)), dma((7,)),
        dma((7,)), dma((7,)),
        dma((7,)), dma((7,)),
        dma((7,)), dma((7,)),
    ]
    out = pl.pallas_call(
        kernel,
        out_shape=(
            jax.ShapeDtypeStruct((T, D), BF),
            jax.ShapeDtypeStruct((T, D), BF),
            jax.ShapeDtypeStruct((T, KV), BF),
            jax.ShapeDtypeStruct((T, KV), BF),
            jax.ShapeDtypeStruct((16, 64), F32),
        ),
        in_specs=[pl.BlockSpec(memory_space=pltpu.SMEM), in_vmem, any_, any_, any_, any_, any_],
        out_specs=(in_vmem,) * 5,
        scratch_shapes=scratch,
        compiler_params=pltpu.CompilerParams(
            collective_id=0, has_side_effects=True, vmem_limit_bytes=40 << 20
        ),
        cost_estimate=pl.CostEstimate(
            flops=1_400_000_000, bytes_accessed=1_500_000, transcendentals=400_000
        ),
        name="sublayer",
    )(
        block_mask[0], patch_order[0], queries[0], keys_in[0], values_in[0], out_weight, cotangent[0]
    )
    mixed, gq, gk, gv, gw = out
    return mixed[None], gq[None], gk[None], gv[None], gw


def solution(mesh):
    tokens = P("dp", "ctx", None)
    in_specs = (tokens, tokens, tokens, tokens, tokens, P("dp", None), tokens)
    out_specs = (tokens, tokens, tokens, tokens, P("dp", "ctx"))
    return jax.shard_map(shards, mesh=mesh, in_specs=in_specs, out_specs=out_specs, check_vma=False)
```

time: 669 us -> 80 us (0.12)
  the two profiles are of different devices: /device:TPU:1 before, /device:TPU:16 now
where the time goes in v1:
time: 80 us; the launch traced here: 79.6 us
  Pallas kernels  70.6 us (88%)
  local copies, waits for them, and re-layouts  8.27 us (10%)
    pallas_call x1, Pallas kernels, shards(): pl.pallas_call(kernel, out_shape=(jax.ShapeDtypeStruct((T, D), BF), jax.S...  70.6 us
    unnamed x19, local copies, waits for them, and re-layouts  8.27 us

profile of v1, /device:TPU:16, one launch (start us, length us, event | category | flops | bytes accessed | tf_op | source)
XLA Modules:
  0.0 79.6 jit_solution(1044750633395505342)
XLA Ops:
  0.6 0.0 copy-start.5
  0.6 0.0 copy-start.6
  0.7 0.7 copy-done.5
  1.3 0.0 copy-done.6
  1.3 0.0 copy-start
  1.3 0.9 %copy-done = bf16[1,128,1024]{2,1,0:T(8,128)(2,1)S(1)} copy-done((bf16[1,128,1024]{2,1,0:T(8,128)(2,1)S(1)}, bf16[1,128,1024]{2,1,0:T(8,128)(2,1)}, u32[]{:S(2)}) %copy-start) | copy-done | bytes 262168
  2.3 0.0 copy-start.1
  2.3 0.9 %copy-done.1 = bf16[1,128,1024]{2,1,0:T(8,128)(2,1)S(1)} copy-done((bf16[1,128,1024]{2,1,0:T(8,128)(2,1)S(1)}, bf16[1,128,1024]{2,1,0:T(8,128)(2,1)}, u32[]{:S(2)}) %copy-start.1) | copy-done | bytes 262168
  3.2 0.0 copy-start.2
  3.2 0.8 %copy-done.2 = bf16[1,128,256]{2,1,0:T(8,128)(2,1)S(1)} copy-done((bf16[1,128,256]{2,1,0:T(8,128)(2,1)S(1)}, bf16[1,128,256]{2,1,0:T(8,128)(2,1)}, u32[]{:S(2)}) %copy-start.2) | copy-done | bytes 65560
  4.1 0.0 copy-start.3
  4.1 0.8 %copy-done.3 = bf16[1,128,256]{2,1,0:T(8,128)(2,1)S(1)} copy-done((bf16[1,128,256]{2,1,0:T(8,128)(2,1)S(1)}, bf16[1,128,256]{2,1,0:T(8,128)(2,1)}, u32[]{:S(2)}) %copy-start.3) | copy-done | bytes 65560
  4.9 0.0 copy-start.4
  4.9 0.8 copy-done.4
  5.7 70.6 %sublayer.1 = (bf16[128,1024]{1,0:T(8,128)(2,1)S(1)}, bf16[128,1024]{1,0:T(8,128)(2,1)S(1)}, bf16[128,256]{1,0:T(8,128)(2,1)S(1)}, bf16[128,256]{1,0:T(8,128)(2,1)S(1)}, f32[16,64]{1,0:T(8,128)S(1)}) custom-call(s32[4,8]{1,0:T(4,128)S(1)} %bitcast.18, s32[1,128]{1,0:T(1,128)S(1)} %bitcast.19, bf16[128,1024]{1,0:T(8,128)(2,1)S(1)} %bitcast.14, ...), custom_call_target="tpu_custom_call" | custom-call | flops 1400000000 | bytes 1500000 | tf_op jit(solution)/shard_map/sublayer/pallas_call | solution.py:343
  76.3 0.7 copy.17
  77.0 0.7 copy.18
  77.7 0.6 copy.19
  78.3 0.6 copy.20
  79.0 0.6 copy.21
Async XLA Ops:
  0.6 0.7 copy-start.5
  0.6 0.7 copy-start.6
  1.3 1.0 %copy-start = (bf16[1,128,1024]{2,1,0:T(8,128)(2,1)S(1)}, bf16[1,128,1024]{2,1,0:T(8,128)(2,1)}, u32[]{:S(2)}) copy-start(bf16[1,128,1024]{2,1,0:T(8,128)(2,1)} %param.7) | copy-start | bytes 786436
  2.3 0.9 %copy-start.1 = (bf16[1,128,1024]{2,1,0:T(8,128)(2,1)S(1)}, bf16[1,128,1024]{2,1,0:T(8,128)(2,1)}, u32[]{:S(2)}) copy-start(bf16[1,128,1024]{2,1,0:T(8,128)(2,1)} %param.13) | copy-start | bytes 786436
  3.2 0.8 %copy-start.2 = (bf16[1,128,256]{2,1,0:T(8,128)(2,1)S(1)}, bf16[1,128,256]{2,1,0:T(8,128)(2,1)}, u32[]{:S(2)}) copy-start(bf16[1,128,256]{2,1,0:T(8,128)(2,1)} %param.8) | copy-start | bytes 196612
  4.1 0.8 %copy-start.3 = (bf16[1,128,256]{2,1,0:T(8,128)(2,1)S(1)}, bf16[1,128,256]{2,1,0:T(8,128)(2,1)}, u32[]{:S(2)}) copy-start(bf16[1,128,256]{2,1,0:T(8,128)(2,1)} %param.9) | copy-start | bytes 196612
  4.9 0.8 copy-start.4

commit v2 on v1

--- a/solution.py
+++ b/solution.py
@@ -18,21 +18,22 @@
 GROUPS = 2
 KV = 256
 BLK = 32
+VMEM_LIMIT = 60 << 20
 D7 = (1, -1, 2, -2, 3, -3, 4)
 NT = (((1,), (1,)), ((), ()))
 NN = (((1,), (0,)), ((), ()))
 
 
 def kernel(
-    mask_s, order_v, q_h, k_h, v_h, w_h, dy_h,
+    order_h, mask_h, q_h, k_h, v_h, w_h, dy_h,
     mixed_o, gq_o, gk_o, gv_o, gw_o,
-    q_v, dy2, kb, vb, order_n, w_full,
+    mask_s, order_v, q_v, dy2, kb, vb, order_n, w_full,
     qst, dast, ktr, vtr, st, pf, pb, dsb, att_t, lhs, att,
     part_k, part_v, got_k, got_v,
-    ga, gb, ra1, rb1, ga2, gb2, ra2, rb2, gy, ry,
+    dyp, ga, gc, ra1, rc1, ga2, gc2, ra2, rc2, gx, rx,
     loc_sem, halo_ss, halo_rs, wz_ss, wz_rs, wx_ss, wx_rs, wc_ss, wc_rs,
     core_ss, core_rs, ph_ss, ph_rs,
-    a1_ss, a1_rs, b1_ss, b1_rs, a2_ss, a2_rs, b2_ss, b2_rs, y_ss, y_rs,
+    a1_ss, a1_rs, c1_ss, c1_rs, a2_ss, a2_rs, c2_ss, c2_rs, x_ss, x_rs,
 ):
     c = lax.axis_index("ctx")
     d = lax.axis_index("dp")
@@ -69,6 +70,8 @@
         pltpu.make_async_copy(v_h, vb.at[1], loc_sem.at[2]),
         pltpu.make_async_copy(dy_h, dy2.at[0], loc_sem.at[3]),
         pltpu.make_async_copy(w_h, w_full.at[z, xl, k], loc_sem.at[4]),
+        pltpu.make_async_copy(order_h, order_v, loc_sem.at[5]),
+        pltpu.make_async_copy(mask_h, mask_s, loc_sem.at[6]),
     ]
     for cp in loc:
         cp.start()
@@ -79,6 +82,8 @@
         friends += [zdev(s), xdev(s), ydev(s)]
     for f in friends:
         pl.semaphore_signal(bar, inc=1, device_id=f, device_id_type=MESH)
+    loc[5].wait()
+    loc[6].wait()
     pl.semaphore_wait(bar, len(friends))
 
     sends = []
@@ -92,9 +97,17 @@
     for i, (s, slot) in enumerate(((1, 0), (-1, 2))):
         halo.append(go(rcopy(k_h, kb.at[slot], halo_ss.at[3 * i], halo_rs.at[3 * i], cdev(s))))
         halo.append(go(rcopy(v_h, vb.at[slot], halo_ss.at[3 * i + 1], halo_rs.at[3 * i + 1], cdev(s))))
-        halo.append(go(rcopy(order_v, order_n.at[i], halo_ss.at[3 * i + 2], halo_rs.at[3 * i + 2], cdev(s))))
+        halo.append(go(rcopy(order_h, order_n.at[i], halo_ss.at[3 * i + 2], halo_rs.at[3 * i + 2], cdev(s))))
     for i, s in enumerate(D7):
         go(rcopy(w_h, w_full.at[z, xl, k], wz_ss.at[i], wz_rs.at[i], zdev(s)))
+    xs = [(1, -1, 2 if j % 2 else -2) for j in range(8)]
+
+    def pass_on(src, j, place):
+        for m, s in enumerate(xs[j]):
+            go(rcopy(src, place, wx_ss.at[3 * j + m], wx_rs.at[3 * j + m], xdev(s)))
+        go(rcopy(src, place, wc_ss.at[j], wc_rs.at[0], mate))
+
+    pass_on(w_h, 0, w_full.at[z, xl, k])
     dy_c = go(rcopy(dy_h, dy2.at[1], core_ss.at[0], core_rs.at[0], mate))
 
     for cp in loc[:3]:
@@ -118,17 +131,19 @@
     jrow = (lax.broadcasted_iota(jnp.int32, (8, T), 1) // BLK).astype(F32).astype(BF)
     q_block = lax.dot_general(jrow, own_hit, NT, preferred_element_type=F32)[0:1]
 
-    loc[4].wait()
     for i, s in enumerate(D7):
         there = w_full.at[(z - s + 8) % 8, xl, k]
         rcopy(w_h, there, wz_ss.at[i], wz_rs.at[i], zdev(s)).wait_recv()
-    column = w_full.at[:, xl, k]
-    go(rcopy(column, column, wx_ss.at[0], wx_rs.at[0], xdev(1)))
-    go(rcopy(column, column, wx_ss.at[1], wx_rs.at[1], xdev(-1)))
-    for i, s in ((2, 2), (3, -2)):
-        part = w_full.at[pl.ds((i - 2) * 4, 4), xl, k]
-        go(rcopy(part, part, wx_ss.at[i], wx_rs.at[i], xdev(s)))
-    go(rcopy(column, column, wc_ss.at[0], wc_rs.at[0], mate))
+        pass_on(there, i + 1, there)
+
+    def order_columns(i):
+        for y_ in range(8):
+            lo = dy2[i, :, y_ * 64 : y_ * 64 + 64]
+            hi = dy2[i, :, 512 + y_ * 64 : 576 + y_ * 64]
+            dyp[i * T : (i + 1) * T, y_ * 128 : (y_ + 1) * 128] = jnp.concatenate([lo, hi], axis=1)
+
+    loc[3].wait()
+    order_columns(0)
 
     for cp in halo:
         cp.wait_recv()
@@ -167,40 +182,32 @@
     for g in range(GROUPS):
         ktr[g] = kb[:, :, g * HD : (g + 1) * HD].reshape(3 * T, HD).T
 
-    loc[3].wait()
     dy_c.wait_recv()
+    order_columns(1)
     lhs[0] = att_t[:, k]
     a_c.wait_recv()
-    left = jnp.concatenate([lhs[0].reshape(512, T), lhs[1].reshape(512, T)], axis=1)
-    right = dy2[...].reshape(2 * T, D)
-    for xh_ in range(2):
-        g_a = jnp.dot(left, right[:, xh_ * 512 : xh_ * 512 + 256], preferred_element_type=F32)
-        ga[:, :, :, xh_ * 256 : (xh_ + 1) * 256] = g_a.astype(BF).reshape(8, 4, 16, 256)
+    left = jnp.concatenate([lhs[0], lhs[1]], axis=2).reshape(8, 4, 16, 2 * T)
+    g_a = jnp.dot(left[:, :2].reshape(256, 2 * T), dyp[...], preferred_element_type=F32)
+    ga[...] = g_a.astype(BF).reshape(8, 2, 16, D)
     a1 = []
     for i, s in enumerate(D7):
         a1.append(go(rcopy(ga.at[(z + s + 8) % 8], ra1.at[i], a1_ss.at[i], a1_rs.at[i], zdev(s))))
-    for xh_ in range(2):
-        g_b = jnp.dot(left, right[:, xh_ * 512 + 256 : xh_ * 512 + 512], preferred_element_type=F32)
-        g_b = g_b.astype(BF).reshape(8, 4, 16, 256)
-        for xl_ in range(4):
-            gb[xh_ * 4 + xl_] = g_b[:, xl_]
-    b1 = []
-    for i, s in enumerate(D7):
-        b1.append(go(rcopy(gb.at[(x + s + 8) % 8], rb1.at[i], b1_ss.at[i], b1_rs.at[i], xdev(s))))
-
-    for i, s in ((0, 1), (1, -1)):
-        there = w_full.at[:, (xl - s + 4) % 4, k]
-        rcopy(there, there, wx_ss.at[i], wx_rs.at[i], xdev(s)).wait_recv()
-        go(rcopy(there, there, wc_ss.at[i + 1], wc_rs.at[i + 1], mate))
-    for i, s in ((2, 2), (3, -2)):
-        there = w_full.at[pl.ds((i - 2) * 4, 4), (xl + 2) % 4, k]
-        rcopy(there, there, wx_ss.at[i], wx_rs.at[i], xdev(s)).wait_recv()
-    there = w_full.at[:, (xl + 2) % 4, k]
-    go(rcopy(there, there, wc_ss.at[3], wc_rs.at[3], mate))
-    for i, s in ((0, 0), (1, -1), (2, 1), (3, 2)):
-        there = w_full.at[:, (xl + s + 4) % 4, other]
-        rcopy(there, there, wc_ss.at[i], wc_rs.at[i], mate).wait_recv()
-
+    g_c = jnp.dot(left[:, 2:].reshape(256, 2 * T), dyp[...], preferred_element_type=F32)
+    for y_ in range(8):
+        gc[y_] = g_c[:, y_ * 128 : (y_ + 1) * 128].astype(BF).reshape(8, 2, 16, 128)
+    c1 = []
+    for i, s in enumerate(D7):
+        c1.append(go(rcopy(gc.at[(y + s + 8) % 8], rc1.at[i], c1_ss.at[i], c1_rs.at[i], ydev(s))))
+
+    for j in range(8):
+        zj = z if j == 0 else (z - D7[j - 1] + 8) % 8
+        for m, s in enumerate(xs[j]):
+            there = w_full.at[zj, (xl - s + 4) % 4, k]
+            rcopy(there, there, wx_ss.at[3 * j + m], wx_rs.at[3 * j + m], xdev(s)).wait_recv()
+            go(rcopy(there, there, wc_ss.at[8 + 3 * j + m], wc_rs.at[0], mate))
+    loc[4].wait()
+    there = w_full.at[:, :, other]
+    rcopy(there, there, wc_ss.at[0], wc_rs.at[0], mate).wait_recv()
     for h in range(8):
         dast[h * T : (h + 1) * T, :] = lax.dot_general(
             dy2[0], w_full[h].reshape(HD, D), NT, preferred_element_type=F32
@@ -229,20 +236,20 @@
     for i in range(7):
         s_a = s_a + ra1[i].astype(F32)
     s_a = s_a.astype(BF)
-    for xh_ in range(2):
-        ga2[xh_ * 4 : (xh_ + 1) * 4] = s_a[:, :, xh_ * 256 : (xh_ + 1) * 256]
+    for y_ in range(8):
+        ga2[y_] = s_a[:, :, y_ * 128 : (y_ + 1) * 128]
     a2 = []
     for i, s in enumerate(D7):
-        a2.append(go(rcopy(ga2.at[(x + s + 8) % 8], ra2.at[i], a2_ss.at[i], a2_rs.at[i], xdev(s))))
-    for cp in b1:
-        cp.wait_recv()
-    s_b = gb[x].astype(F32)
+        a2.append(go(rcopy(ga2.at[(y + s + 8) % 8], ra2.at[i], a2_ss.at[i], a2_rs.at[i], ydev(s))))
+    for cp in c1:
+        cp.wait_recv()
+    s_c = gc[y].astype(F32)
     for i in range(7):
-        s_b = s_b + rb1[i].astype(F32)
-    gb2[...] = s_b.astype(BF)
-    b2 = []
-    for i, s in enumerate(D7):
-        b2.append(go(rcopy(gb2.at[(z + s + 8) % 8], rb2.at[i], b2_ss.at[i], b2_rs.at[i], zdev(s))))
+        s_c = s_c + rc1[i].astype(F32)
+    gc2[...] = s_c.astype(BF)
+    c2 = []
+    for i, s in enumerate(D7):
+        c2.append(go(rcopy(gc2.at[(z + s + 8) % 8], rc2.at[i], c2_ss.at[i], c2_rs.at[i], zdev(s))))
 
     mixed_o[...] = jnp.dot(
         att[...], w_full[...].reshape(D, D), preferred_element_type=F32
@@ -255,22 +262,20 @@
 
     for cp in a2:
         cp.wait_recv()
-    f_a = ga2[x].astype(F32)
+    f_a = ga2[y].astype(F32)
     for i in range(7):
         f_a = f_a + ra2[i].astype(F32)
-    gy[0] = f_a[:, :128]
-    gy[1] = f_a[:, 128:]
-    for cp in b2:
-        cp.wait_recv()
-    f_b = gb2[z].astype(F32)
+    gx[0:2] = f_a
+    for cp in c2:
+        cp.wait_recv()
+    f_c = gc2[z].astype(F32)
     for i in range(7):
-        f_b = f_b + rb2[i].astype(F32)
-    gy[2] = f_b[:, :128]
-    gy[3] = f_b[:, 128:]
+        f_c = f_c + rc2[i].astype(F32)
+    gx[2:4] = f_c
     legs = []
     for i, s in enumerate(D7):
-        to = (y + s + 8) % 8
-        legs.append(go(rcopy(gy.at[to // 2], ry.at[i], y_ss.at[i], y_rs.at[i], ydev(s))))
+        to = (xl + s + 8) % 4
+        legs.append(go(rcopy(gx.at[to], rx.at[i], x_ss.at[i], x_rs.at[i], xdev(s))))
 
     for cp in part:
         cp.wait_recv()
@@ -279,23 +284,38 @@
 
     for cp in legs:
         cp.wait_recv()
-    total = gy[y // 2]
+    total = gx[xl]
     for i in range(7):
-        total = total + ry[i]
+        total = total + rx[i]
     norm = 1.0 / math.sqrt(64 * 16 * T)
-    odd = jnp.full((16, 64), y % 2, jnp.int32) > 0
-    gw_o[...] = jnp.where(odd, total[:, 64:], total[:, :64]) * norm
+    high = jnp.full((16, 64), xh, jnp.int32) > 0
+    gw_o[...] = jnp.where(high, total[:, 64:], total[:, :64]) * norm
 
     for cp in sends:
         cp.wait_send()
+
+
+def store(*refs):
+    ins, outs, room, sem = refs[:5], refs[5:10], refs[10:15], refs[15]
+    loads = [pltpu.make_async_copy(ins[i], room[i], sem.at[i]) for i in range(5)]
+    saves = [pltpu.make_async_copy(room[i], outs[i], sem.at[5 + i]) for i in range(5)]
+    for cp in loads:
+        cp.start()
+    for load, save in zip(loads, saves):
+        load.wait()
+        save.start()
+    for cp in saves:
+        cp.wait()
 
 
 def shards(queries, keys_in, values_in, patch_order, block_mask, out_weight, cotangent):
     dma = pltpu.SemaphoreType.DMA
     vm = pltpu.VMEM
-    any_ = pl.BlockSpec(memory_space=pl.ANY)
+    hbm = pl.BlockSpec(memory_space=pltpu.HBM)
     in_vmem = pl.BlockSpec(memory_space=pltpu.VMEM)
     scratch = [
+        pltpu.SMEM((4, 8), jnp.int32),
+        vm((1, T), jnp.int32),
         vm((T, D), BF),
         vm((2, T, D), BF),
         vm((3, T, KV), BF),
@@ -317,21 +337,22 @@
         vm((3, T, KV), BF),
         vm((2, T, KV), BF),
         vm((2, T, KV), BF),
-        vm((8, 4, 16, 512), BF),
-        vm((8, 8, 16, 256), BF),
-        vm((7, 4, 16, 512), BF),
-        vm((7, 8, 16, 256), BF),
-        vm((8, 16, 256), BF),
-        vm((8, 16, 256), BF),
-        vm((7, 16, 256), BF),
-        vm((7, 16, 256), BF),
+        vm((2 * T, D), BF),
+        vm((8, 2, 16, D), BF),
+        vm((8, 8, 2, 16, 128), BF),
+        vm((7, 2, 16, D), BF),
+        vm((7, 8, 2, 16, 128), BF),
+        vm((8, 2, 16, 128), BF),
+        vm((8, 2, 16, 128), BF),
+        vm((7, 2, 16, 128), BF),
+        vm((7, 2, 16, 128), BF),
         vm((4, 16, 128), F32),
         vm((7, 16, 128), F32),
-        dma((5,)),
+        dma((7,)),
         dma((6,)), dma((6,)),
         dma((7,)), dma((7,)),
-        dma((4,)), dma((4,)),
-        dma((4,)), dma((4,)),
+        dma((24,)), dma((24,)),
+        dma((32,)), dma((1,)),
         dma((2,)), dma((2,)),
         dma((4,)), dma((4,)),
         dma((7,)), dma((7,)),
@@ -349,20 +370,28 @@
             jax.ShapeDtypeStruct((T, KV), BF),
             jax.ShapeDtypeStruct((16, 64), F32),
         ),
-        in_specs=[pl.BlockSpec(memory_space=pltpu.SMEM), in_vmem, any_, any_, any_, any_, any_],
+        in_specs=[hbm] * 7,
         out_specs=(in_vmem,) * 5,
         scratch_shapes=scratch,
         compiler_params=pltpu.CompilerParams(
-            collective_id=0, has_side_effects=True, vmem_limit_bytes=40 << 20
+            collective_id=0, has_side_effects=True, vmem_limit_bytes=VMEM_LIMIT
         ),
         cost_estimate=pl.CostEstimate(
             flops=1_400_000_000, bytes_accessed=1_500_000, transcendentals=400_000
         ),
         name="sublayer",
     )(
-        block_mask[0], patch_order[0], queries[0], keys_in[0], values_in[0], out_weight, cotangent[0]
+        patch_order[0], block_mask[0], queries[0], keys_in[0], values_in[0], out_weight, cotangent[0]
     )
-    mixed, gq, gk, gv, gw = out
+    mixed, gq, gk, gv, gw = pl.pallas_call(
+        store,
+        out_shape=[jax.ShapeDtypeStruct(o.shape, o.dtype) for o in out],
+        in_specs=[hbm] * 5,
+        out_specs=[hbm] * 5,
+        scratch_shapes=[vm(o.shape, o.dtype) for o in out] + [dma((10,))],
+        compiler_params=pltpu.CompilerParams(vmem_limit_bytes=VMEM_LIMIT),
+        name="store",
+    )(*out)
     return mixed[None], gq[None], gk[None], gv[None], gw
 
 

time: 80 us -> 67.8 us (0.85)
  the two profiles are of different devices: /device:TPU:16 before, /device:TPU:32 now
where the time goes in v2:
time: 67.8 us; the launch traced here: 67.6 us
  Pallas kernels  67 us (99%)
    pallas_call x1, Pallas kernels, shards(): pl.pallas_call(kernel, out_shape=(jax.ShapeDtypeStruct((T, D), BF), jax.S...  65.1 us
    pallas_call x1, Pallas kernels, shards(): pl.pallas_call(store, out_shape=[jax.ShapeDtypeStruct(o.shape, o.dtype) f...  1.86 us

profile of v2, /device:TPU:32, one launch (start us, length us, event | category | flops | bytes accessed | tf_op | source)
XLA Modules:
  0.0 67.6 jit_solution(4017825660376104124)
XLA Ops:
  0.6 65.1 %sublayer.1 = (bf16[128,1024]{1,0:T(8,128)(2,1)}, bf16[128,1024]{1,0:T(8,128)(2,1)}, bf16[128,256]{1,0:T(8,128)(2,1)}, bf16[128,256]{1,0:T(8,128)(2,1)}, f32[16,64]{1,0:T(8,128)}) custom-call(s32[1,128]{1,0:T(1,128)} %bitcast.19, s32[4,8]{1,0:T(4,128)} %bitcast.18, bf16[128,1024]{1,0:T(8,128)(2,1)} %bitcast.10, bf16[128,256]{1,0:T(8,128)(2,1)} %bitcast.14, ...), custom_call_target="tpu_custom_call" | custom-call | flops 1400000000 | bytes 1500000 | tf_op jit(solution)/shard_map/sublayer/pallas_call | solution.py:364
  65.8 1.9 %store.1 = (bf16[128,1024]{1,0:T(8,128)(2,1)}, bf16[128,1024]{1,0:T(8,128)(2,1)}, bf16[128,256]{1,0:T(8,128)(2,1)}, bf16[128,256]{1,0:T(8,128)(2,1)}, f32[16,64]{1,0:T(8,128)}) custom-call(bf16[128,1024]{1,0:T(8,128)(2,1)} %get-tuple-element.15.refs_0_, bf16[128,1024]{1,0:T(8,128)(2,1)} %get-tuple-element.16.refs_1_, ...), custom_call_target="tpu_custom_call" | custom-call | tf_op jit(solution)/shard_map/store/pallas_call | solution.py:386

commit v3 on v2

--- a/solution.py
+++ b/solution.py
@@ -26,7 +26,8 @@
 
 def kernel(
     order_h, mask_h, q_h, k_h, v_h, w_h, dy_h,
-    mixed_o, gq_o, gk_o, gv_o, gw_o,
+    mixed_h, gq_h, gk_h, gv_h, gw_h,
+    mixed_o, gq_o, gk_o, gv_o, gw_o, out_sem,
     mask_s, order_v, q_v, dy2, kb, vb, order_n, w_full,
     qst, dast, ktr, vtr, st, pf, pb, dsb, att_t, lhs, att,
     part_k, part_v, got_k, got_v,
@@ -87,6 +88,12 @@
     pl.semaphore_wait(bar, len(friends))
 
     sends = []
+    saves = []
+
+    def save(i, src, dst):
+        cp = pltpu.make_async_copy(src, dst, out_sem.at[i])
+        cp.start()
+        saves.append(cp)
 
     def go(cp):
         cp.start()
@@ -100,14 +107,6 @@
         halo.append(go(rcopy(order_h, order_n.at[i], halo_ss.at[3 * i + 2], halo_rs.at[3 * i + 2], cdev(s))))
     for i, s in enumerate(D7):
         go(rcopy(w_h, w_full.at[z, xl, k], wz_ss.at[i], wz_rs.at[i], zdev(s)))
-    xs = [(1, -1, 2 if j % 2 else -2) for j in range(8)]
-
-    def pass_on(src, j, place):
-        for m, s in enumerate(xs[j]):
-            go(rcopy(src, place, wx_ss.at[3 * j + m], wx_rs.at[3 * j + m], xdev(s)))
-        go(rcopy(src, place, wc_ss.at[j], wc_rs.at[0], mate))
-
-    pass_on(w_h, 0, w_full.at[z, xl, k])
     dy_c = go(rcopy(dy_h, dy2.at[1], core_ss.at[0], core_rs.at[0], mate))
 
     for cp in loc[:3]:
@@ -130,11 +129,6 @@
     own_hit = (irow == jnp.broadcast_to(order_v[...], (T, T))).astype(F32).astype(BF)
     jrow = (lax.broadcasted_iota(jnp.int32, (8, T), 1) // BLK).astype(F32).astype(BF)
     q_block = lax.dot_general(jrow, own_hit, NT, preferred_element_type=F32)[0:1]
-
-    for i, s in enumerate(D7):
-        there = w_full.at[(z - s + 8) % 8, xl, k]
-        rcopy(w_h, there, wz_ss.at[i], wz_rs.at[i], zdev(s)).wait_recv()
-        pass_on(there, i + 1, there)
 
     def order_columns(i):
         for y_ in range(8):
@@ -179,9 +173,16 @@
             att_t[h * 4 : (h + 1) * 4] = at[:, j * T : (j + 1) * T].reshape(4, 2, 16, T)
             att[:, h * HD : (h + 1) * HD] = at[:, j * T : (j + 1) * T].T
     a_c = go(rcopy(att_t.at[:, other], lhs.at[1], core_ss.at[1], core_rs.at[1], mate))
-    for g in range(GROUPS):
-        ktr[g] = kb[:, :, g * HD : (g + 1) * HD].reshape(3 * T, HD).T
-
+    loc[4].wait()
+    for i, s in enumerate(D7):
+        there = w_full.at[(z - s + 8) % 8, xl, k]
+        rcopy(w_h, there, wz_ss.at[i], wz_rs.at[i], zdev(s)).wait_recv()
+    legs_w = ((1, 0), (-1, 0), (2, 0), (1, 1), (-1, 1), (-2, 1))
+    for i, (s, half) in enumerate(legs_w):
+        rows = w_full.at[pl.ds(half * 4, 4), xl, k]
+        go(rcopy(rows, rows, wx_ss.at[i], wx_rs.at[i], xdev(s)))
+    column = w_full.at[:, xl, k]
+    go(rcopy(column, column, wc_ss.at[0], wc_rs.at[0], mate))
     dy_c.wait_recv()
     order_columns(1)
     lhs[0] = att_t[:, k]
@@ -199,13 +200,12 @@
     for i, s in enumerate(D7):
         c1.append(go(rcopy(gc.at[(y + s + 8) % 8], rc1.at[i], c1_ss.at[i], c1_rs.at[i], ydev(s))))
 
-    for j in range(8):
-        zj = z if j == 0 else (z - D7[j - 1] + 8) % 8
-        for m, s in enumerate(xs[j]):
-            there = w_full.at[zj, (xl - s + 4) % 4, k]
-            rcopy(there, there, wx_ss.at[3 * j + m], wx_rs.at[3 * j + m], xdev(s)).wait_recv()
-            go(rcopy(there, there, wc_ss.at[8 + 3 * j + m], wc_rs.at[0], mate))
-    loc[4].wait()
+    for g in range(GROUPS):
+        ktr[g] = kb[:, :, g * HD : (g + 1) * HD].reshape(3 * T, HD).T
+    for i, (s, half) in enumerate(legs_w):
+        there = w_full.at[pl.ds(half * 4, 4), (xl - s + 4) % 4, k]
+        rcopy(there, there, wx_ss.at[i], wx_rs.at[i], xdev(s)).wait_recv()
+        go(rcopy(there, there, wc_ss.at[1 + i], wc_rs.at[0], mate))
     there = w_full.at[:, :, other]
     rcopy(there, there, wc_ss.at[0], wc_rs.at[0], mate).wait_recv()
     for h in range(8):
@@ -260,6 +260,8 @@
             h = g * GROUP + j
             gq_o[:, h * HD : (h + 1) * HD] = gq[:, j * T : (j + 1) * T].astype(BF).T
 
+    save(0, mixed_o, mixed_h)
+    save(1, gq_o, gq_h)
     for cp in a2:
         cp.wait_recv()
     f_a = ga2[y].astype(F32)
@@ -282,6 +284,8 @@
     gv_o[...] = (part_v[1].astype(F32) + got_v[0].astype(F32) + got_v[1].astype(F32)).astype(BF)
     gk_o[...] = (part_k[1].astype(F32) + got_k[0].astype(F32) + got_k[1].astype(F32)).astype(BF)
 
+    save(2, gk_o, gk_h)
+    save(3, gv_o, gv_h)
     for cp in legs:
         cp.wait_recv()
     total = gx[xl]
@@ -291,8 +295,11 @@
     high = jnp.full((16, 64), xh, jnp.int32) > 0
     gw_o[...] = jnp.where(high, total[:, 64:], total[:, :64]) * norm
 
+    save(4, gw_o, gw_h)
     for cp in sends:
         cp.wait_send()
+    for cp in saves:
+        cp.wait()
 
 
 def store(*refs):
@@ -312,8 +319,13 @@
     dma = pltpu.SemaphoreType.DMA
     vm = pltpu.VMEM
     hbm = pl.BlockSpec(memory_space=pltpu.HBM)
-    in_vmem = pl.BlockSpec(memory_space=pltpu.VMEM)
     scratch = [
+        vm((T, D), BF),
+        vm((T, D), BF),
+        vm((T, KV), BF),
+        vm((T, KV), BF),
+        vm((16, 64), F32),
+        dma((5,)),
         pltpu.SMEM((4, 8), jnp.int32),
         vm((1, T), jnp.int32),
         vm((T, D), BF),
@@ -351,8 +363,8 @@
         dma((7,)),
         dma((6,)), dma((6,)),
         dma((7,)), dma((7,)),
-        dma((24,)), dma((24,)),
-        dma((32,)), dma((1,)),
+        dma((6,)), dma((6,)),
+        dma((7,)), dma((1,)),
         dma((2,)), dma((2,)),
         dma((4,)), dma((4,)),
         dma((7,)), dma((7,)),
@@ -371,7 +383,7 @@
             jax.ShapeDtypeStruct((16, 64), F32),
         ),
         in_specs=[hbm] * 7,
-        out_specs=(in_vmem,) * 5,
+        out_specs=(hbm,) * 5,
         scratch_shapes=scratch,
         compiler_params=pltpu.CompilerParams(
             collective_id=0, has_side_effects=True, vmem_limit_bytes=VMEM_LIMIT

time: 67.8 us -> 65.4 us (0.965)
  the two profiles are of different devices: /device:TPU:32 before, /device:TPU:1 now
where the time goes in v3:
time: 65.4 us; the launch traced here: 65.2 us
  Pallas kernels  64.6 us (99%)
    pallas_call x1, Pallas kernels, shards(): pl.pallas_call(kernel, out_shape=(jax.ShapeDtypeStruct((T, D), BF), jax.S...  62.7 us
    pallas_call x1, Pallas kernels, shards(): pl.pallas_call(store, out_shape=[jax.ShapeDtypeStruct(o.shape, o.dtype) f...  1.86 us

profile of v3, /device:TPU:1, one launch (start us, length us, event | category | flops | bytes accessed | tf_op | source)
XLA Modules:
  0.0 65.2 jit_solution(6215555750065032920)
XLA Ops:
  0.6 62.7 %sublayer.1 = (bf16[128,1024]{1,0:T(8,128)(2,1)}, bf16[128,1024]{1,0:T(8,128)(2,1)}, bf16[128,256]{1,0:T(8,128)(2,1)}, bf16[128,256]{1,0:T(8,128)(2,1)}, f32[16,64]{1,0:T(8,128)}) custom-call(s32[1,128]{1,0:T(1,128)} %bitcast.19, s32[4,8]{1,0:T(4,128)} %bitcast.18, bf16[128,1024]{1,0:T(8,128)(2,1)} %bitcast.10, bf16[128,256]{1,0:T(8,128)(2,1)} %bitcast.14, ...), custom_call_target="tpu_custom_call" | custom-call | flops 1400000000 | bytes 1500000 | tf_op jit(solution)/shard_map/sublayer/pallas_call | solution.py:376
  63.4 1.9 %store.1 = (bf16[128,1024]{1,0:T(8,128)(2,1)}, bf16[128,1024]{1,0:T(8,128)(2,1)}, bf16[128,256]{1,0:T(8,128)(2,1)}, bf16[128,256]{1,0:T(8,128)(2,1)}, f32[16,64]{1,0:T(8,128)}) custom-call(bf16[128,1024]{1,0:T(8,128)(2,1)} %get-tuple-element.15.refs_0_, bf16[128,1024]{1,0:T(8,128)(2,1)} %get-tuple-element.16.refs_1_, ...), custom_call_target="tpu_custom_call" | custom-call | tf_op jit(solution)/shard_map/store/pallas_call | solution.py:398

commit v4 on v3

--- a/solution.py
+++ b/solution.py
@@ -19,15 +19,14 @@
 KV = 256
 BLK = 32
 VMEM_LIMIT = 60 << 20
-D7 = (1, -1, 2, -2, 3, -3, 4)
+D7 = (4, 3, -3, 2, -2, 1, -1)
 NT = (((1,), (1,)), ((), ()))
 NN = (((1,), (0,)), ((), ()))
 
 
 def kernel(
     order_h, mask_h, q_h, k_h, v_h, w_h, dy_h,
-    mixed_h, gq_h, gk_h, gv_h, gw_h,
-    mixed_o, gq_o, gk_o, gv_o, gw_o, out_sem,
+    mixed_o, gq_o, gk_o, gv_o, gw_o,
     mask_s, order_v, q_v, dy2, kb, vb, order_n, w_full,
     qst, dast, ktr, vtr, st, pf, pb, dsb, att_t, lhs, att,
     part_k, part_v, got_k, got_v,
@@ -88,23 +87,18 @@
     pl.semaphore_wait(bar, len(friends))
 
     sends = []
-    saves = []
-
-    def save(i, src, dst):
-        cp = pltpu.make_async_copy(src, dst, out_sem.at[i])
-        cp.start()
-        saves.append(cp)
-
     def go(cp):
         cp.start()
         sends.append(cp)
         return cp
 
-    halo = []
-    for i, (s, slot) in enumerate(((1, 0), (-1, 2))):
+    halo, halo_v = [], []
+    sides = ((1, 0), (-1, 2))
+    for i, (s, slot) in enumerate(sides):
         halo.append(go(rcopy(k_h, kb.at[slot], halo_ss.at[3 * i], halo_rs.at[3 * i], cdev(s))))
-        halo.append(go(rcopy(v_h, vb.at[slot], halo_ss.at[3 * i + 1], halo_rs.at[3 * i + 1], cdev(s))))
         halo.append(go(rcopy(order_h, order_n.at[i], halo_ss.at[3 * i + 2], halo_rs.at[3 * i + 2], cdev(s))))
+    for i, (s, slot) in enumerate(sides):
+        halo_v.append(go(rcopy(v_h, vb.at[slot], halo_ss.at[3 * i + 1], halo_rs.at[3 * i + 1], cdev(s))))
     for i, s in enumerate(D7):
         go(rcopy(w_h, w_full.at[z, xl, k], wz_ss.at[i], wz_rs.at[i], zdev(s)))
     dy_c = go(rcopy(dy_h, dy2.at[1], core_ss.at[0], core_rs.at[0], mate))
@@ -165,6 +159,9 @@
         p = e * (1.0 / jnp.sum(e, axis=0, keepdims=True))
         pf[g] = p
         pb[g] = p.astype(BF)
+    for cp in halo_v:
+        cp.wait_recv()
+    for g in range(GROUPS):
         v_g = vb[:, :, g * HD : (g + 1) * HD].reshape(3 * T, HD)
         vtr[g] = v_g.T
         at = jnp.dot(vtr[g], pb[g], preferred_element_type=F32).astype(BF)
@@ -260,8 +257,6 @@
             h = g * GROUP + j
             gq_o[:, h * HD : (h + 1) * HD] = gq[:, j * T : (j + 1) * T].astype(BF).T
 
-    save(0, mixed_o, mixed_h)
-    save(1, gq_o, gq_h)
     for cp in a2:
         cp.wait_recv()
     f_a = ga2[y].astype(F32)
@@ -284,8 +279,6 @@
     gv_o[...] = (part_v[1].astype(F32) + got_v[0].astype(F32) + got_v[1].astype(F32)).astype(BF)
     gk_o[...] = (part_k[1].astype(F32) + got_k[0].astype(F32) + got_k[1].astype(F32)).astype(BF)
 
-    save(2, gk_o, gk_h)
-    save(3, gv_o, gv_h)
     for cp in legs:
         cp.wait_recv()
     total = gx[xl]
@@ -295,22 +288,14 @@
     high = jnp.full((16, 64), xh, jnp.int32) > 0
     gw_o[...] = jnp.where(high, total[:, 64:], total[:, :64]) * norm
 
-    save(4, gw_o, gw_h)
     for cp in sends:
         cp.wait_send()
+
+
+def store(*refs):
+    saves = [pltpu.make_async_copy(refs[i], refs[5 + i], refs[10].at[i]) for i in range(5)]
     for cp in saves:
-        cp.wait()
-
-
-def store(*refs):
-    ins, outs, room, sem = refs[:5], refs[5:10], refs[10:15], refs[15]
-    loads = [pltpu.make_async_copy(ins[i], room[i], sem.at[i]) for i in range(5)]
-    saves = [pltpu.make_async_copy(room[i], outs[i], sem.at[5 + i]) for i in range(5)]
-    for cp in loads:
         cp.start()
-    for load, save in zip(loads, saves):
-        load.wait()
-        save.start()
     for cp in saves:
         cp.wait()
 
@@ -319,13 +304,8 @@
     dma = pltpu.SemaphoreType.DMA
     vm = pltpu.VMEM
     hbm = pl.BlockSpec(memory_space=pltpu.HBM)
+    in_vmem = pl.BlockSpec(memory_space=pltpu.VMEM)
     scratch = [
-        vm((T, D), BF),
-        vm((T, D), BF),
-        vm((T, KV), BF),
-        vm((T, KV), BF),
-        vm((16, 64), F32),
-        dma((5,)),
         pltpu.SMEM((4, 8), jnp.int32),
         vm((1, T), jnp.int32),
         vm((T, D), BF),
@@ -376,14 +356,14 @@
     out = pl.pallas_call(
         kernel,
         out_shape=(
-            jax.ShapeDtypeStruct((T, D), BF),
-            jax.ShapeDtypeStruct((T, D), BF),
-            jax.ShapeDtypeStruct((T, KV), BF),
-            jax.ShapeDtypeStruct((T, KV), BF),
-            jax.ShapeDtypeStruct((16, 64), F32),
+            vm((T, D), BF),
+            vm((T, D), BF),
+            vm((T, KV), BF),
+            vm((T, KV), BF),
+            vm((16, 64), F32),
         ),
         in_specs=[hbm] * 7,
-        out_specs=(hbm,) * 5,
+        out_specs=(in_vmem,) * 5,
         scratch_shapes=scratch,
         compiler_params=pltpu.CompilerParams(
             collective_id=0, has_side_effects=True, vmem_limit_bytes=VMEM_LIMIT
@@ -398,10 +378,10 @@
     mixed, gq, gk, gv, gw = pl.pallas_call(
         store,
         out_shape=[jax.ShapeDtypeStruct(o.shape, o.dtype) for o in out],
-        in_specs=[hbm] * 5,
+        in_specs=[in_vmem] * 5,
         out_specs=[hbm] * 5,
-        scratch_shapes=[vm(o.shape, o.dtype) for o in out] + [dma((10,))],
-        compiler_params=pltpu.CompilerParams(vmem_limit_bytes=VMEM_LIMIT),
+        scratch_shapes=[dma((5,))],
+        compiler_params=pltpu.CompilerParams(vmem_limit_bytes=4 << 20),
         name="store",
     )(*out)
     return mixed[None], gq[None], gk[None], gv[None], gw

time: 65.4 us -> 62.1 us (0.950)
  Pallas kernels: 64.6 us -> 61.3 us
    pallas_call x1, Pallas kernels: 62.7 us -> 60.4 us  [shards(): pl.pallas_call(kernel, out_shape=(vm((T, D), BF), vm((T, D), BF), vm((T,...]
    pallas_call x1, Pallas kernels: 1.86 us -> 0.87 us  [shards(): pl.pallas_call(store, out_shape=[jax.ShapeDtypeStruct(o.shape, o.dtype) f...]
where the time goes in v4:
time: 62.1 us; the launch traced here: 61.9 us
  Pallas kernels  61.3 us (99%)
  between operations  0.64 us (1%)
    pallas_call x1, Pallas kernels, shards(): pl.pallas_call(kernel, out_shape=(vm((T, D), BF), vm((T, D), BF), vm((T,...  60.4 us

profile of v4, /device:TPU:1, one launch (start us, length us, event | category | flops | bytes accessed | tf_op | source)
XLA Modules:
  0.0 61.9 jit_solution(4397189421262051629)
XLA Ops:
  0.6 60.4 %sublayer.1 = (bf16[128,1024]{1,0:T(8,128)(2,1)S(1)}, bf16[128,1024]{1,0:T(8,128)(2,1)S(1)}, bf16[128,256]{1,0:T(8,128)(2,1)S(1)}, bf16[128,256]{1,0:T(8,128)(2,1)S(1)}, f32[16,64]{1,0:T(8,128)S(1)}) custom-call(s32[1,128]{1,0:T(1,128)} %bitcast.19, s32[4,8]{1,0:T(4,128)} %bitcast.18, bf16[128,1024]{1,0:T(8,128)(2,1)} %bitcast.10, ...), custom_call_target="tpu_custom_call" | custom-call | flops 1400000000 | bytes 1500000 | tf_op jit(solution)/shard_map/sublayer/pallas_call | solution.py:356
  61.0 0.9 %store.1 = (bf16[128,1024]{1,0:T(8,128)(2,1)}, bf16[128,1024]{1,0:T(8,128)(2,1)}, bf16[128,256]{1,0:T(8,128)(2,1)}, bf16[128,256]{1,0:T(8,128)(2,1)}, f32[16,64]{1,0:T(8,128)}) custom-call(bf16[128,1024]{1,0:T(8,128)(2,1)S(1)} %get-tuple-element.15.refs_0_, bf16[128,1024]{1,0:T(8,128)(2,1)S(1)} %get-tuple-element.16.refs_1_, ...), custom_call_target="tpu_custom_call" | custom-call | tf_op jit(solution)/shard_map/store/pallas_call | solution.py:378

commit v5 on v4

--- a/solution.py
+++ b/solution.py
@@ -20,6 +20,7 @@
 BLK = 32
 VMEM_LIMIT = 60 << 20
 D7 = (4, 3, -3, 2, -2, 1, -1)
+NEAR_FIRST = (5, 6, 3, 4, 1, 2, 0)
 NT = (((1,), (1,)), ((), ()))
 NN = (((1,), (0,)), ((), ()))
 
@@ -174,7 +175,7 @@
     for i, s in enumerate(D7):
         there = w_full.at[(z - s + 8) % 8, xl, k]
         rcopy(w_h, there, wz_ss.at[i], wz_rs.at[i], zdev(s)).wait_recv()
-    legs_w = ((1, 0), (-1, 0), (2, 0), (1, 1), (-1, 1), (-2, 1))
+    legs_w = ((2, 0), (-2, 1), (1, 0), (-1, 0), (1, 1), (-1, 1))
     for i, (s, half) in enumerate(legs_w):
         rows = w_full.at[pl.ds(half * 4, 4), xl, k]
         go(rcopy(rows, rows, wx_ss.at[i], wx_rs.at[i], xdev(s)))
@@ -227,10 +228,9 @@
     part.append(go(rcopy(part_k.at[0], got_k.at[0], ph_ss.at[2], ph_rs.at[2], cdev(-1))))
     part.append(go(rcopy(part_k.at[2], got_k.at[1], ph_ss.at[3], ph_rs.at[3], cdev(1))))
 
-    for cp in a1:
-        cp.wait_recv()
     s_a = ga[z].astype(F32)
-    for i in range(7):
+    for i in NEAR_FIRST:
+        a1[i].wait_recv()
         s_a = s_a + ra1[i].astype(F32)
     s_a = s_a.astype(BF)
     for y_ in range(8):
@@ -238,10 +238,9 @@
     a2 = []
     for i, s in enumerate(D7):
         a2.append(go(rcopy(ga2.at[(y + s + 8) % 8], ra2.at[i], a2_ss.at[i], a2_rs.at[i], ydev(s))))
-    for cp in c1:
-        cp.wait_recv()
     s_c = gc[y].astype(F32)
-    for i in range(7):
+    for i in NEAR_FIRST:
+        c1[i].wait_recv()
         s_c = s_c + rc1[i].astype(F32)
     gc2[...] = s_c.astype(BF)
     c2 = []
@@ -257,16 +256,14 @@
             h = g * GROUP + j
             gq_o[:, h * HD : (h + 1) * HD] = gq[:, j * T : (j + 1) * T].astype(BF).T
 
-    for cp in a2:
-        cp.wait_recv()
     f_a = ga2[y].astype(F32)
-    for i in range(7):
+    for i in NEAR_FIRST:
+        a2[i].wait_recv()
         f_a = f_a + ra2[i].astype(F32)
     gx[0:2] = f_a
-    for cp in c2:
-        cp.wait_recv()
     f_c = gc2[z].astype(F32)
-    for i in range(7):
+    for i in NEAR_FIRST:
+        c2[i].wait_recv()
         f_c = f_c + rc2[i].astype(F32)
     gx[2:4] = f_c
     legs = []
@@ -279,10 +276,9 @@
     gv_o[...] = (part_v[1].astype(F32) + got_v[0].astype(F32) + got_v[1].astype(F32)).astype(BF)
     gk_o[...] = (part_k[1].astype(F32) + got_k[0].astype(F32) + got_k[1].astype(F32)).astype(BF)
 
-    for cp in legs:
-        cp.wait_recv()
     total = gx[xl]
-    for i in range(7):
+    for i in NEAR_FIRST:
+        legs[i].wait_recv()
         total = total + rx[i]
     norm = 1.0 / math.sqrt(64 * 16 * T)
     high = jnp.full((16, 64), xh, jnp.int32) > 0

time: 62.1 us -> 61.6 us (level)
  no operation moved by 1% of the time
where the time goes in v5:
time: 61.6 us; the launch traced here: 61.5 us
  Pallas kernels  60.8 us (99%)
  between operations  0.64 us (1%)
    pallas_call x1, Pallas kernels, shards(): pl.pallas_call(kernel, out_shape=(vm((T, D), BF), vm((T, D), BF), vm((T,...  60 us

profile of v5, /device:TPU:1, one launch (start us, length us, event | category | flops | bytes accessed | tf_op | source)
XLA Modules:
  0.0 61.5 jit_solution(5359069646221937448)
XLA Ops:
  0.6 60.0 %sublayer.1 = (bf16[128,1024]{1,0:T(8,128)(2,1)S(1)}, bf16[128,1024]{1,0:T(8,128)(2,1)S(1)}, bf16[128,256]{1,0:T(8,128)(2,1)S(1)}, bf16[128,256]{1,0:T(8,128)(2,1)S(1)}, f32[16,64]{1,0:T(8,128)S(1)}) custom-call(s32[1,128]{1,0:T(1,128)} %bitcast.19, s32[4,8]{1,0:T(4,128)} %bitcast.18, bf16[128,1024]{1,0:T(8,128)(2,1)} %bitcast.10, ...), custom_call_target="tpu_custom_call" | custom-call | flops 1400000000 | bytes 1500000 | tf_op jit(solution)/shard_map/sublayer/pallas_call | solution.py:352
  60.6 0.9 %store.1 = (bf16[128,1024]{1,0:T(8,128)(2,1)}, bf16[128,1024]{1,0:T(8,128)(2,1)}, bf16[128,256]{1,0:T(8,128)(2,1)}, bf16[128,256]{1,0:T(8,128)(2,1)}, f32[16,64]{1,0:T(8,128)}) custom-call(bf16[128,1024]{1,0:T(8,128)(2,1)S(1)} %get-tuple-element.15.refs_0_, bf16[128,1024]{1,0:T(8,128)(2,1)S(1)} %get-tuple-element.16.refs_1_, ...), custom_call_target="tpu_custom_call" | custom-call | tf_op jit(solution)/shard_map/store/pallas_call | solution.py:374

commit v6 on v5

--- a/solution.py
+++ b/solution.py
@@ -78,9 +78,10 @@
         cp.start()
 
     bar = pltpu.get_barrier_semaphore()
-    friends = [cdev(1), cdev(-1), mate]
+    friends = []
     for s in D7:
         friends += [zdev(s), xdev(s), ydev(s)]
+    friends += [cdev(1), cdev(-1), mate]
     for f in friends:
         pl.semaphore_signal(bar, inc=1, device_id=f, device_id_type=MESH)
     loc[5].wait()
@@ -162,6 +163,7 @@
         pb[g] = p.astype(BF)
     for cp in halo_v:
         cp.wait_recv()
+    a_c = []
     for g in range(GROUPS):
         v_g = vb[:, :, g * HD : (g + 1) * HD].reshape(3 * T, HD)
         vtr[g] = v_g.T
@@ -170,7 +172,11 @@
             h = g * GROUP + j
             att_t[h * 4 : (h + 1) * 4] = at[:, j * T : (j + 1) * T].reshape(4, 2, 16, T)
             att[:, h * HD : (h + 1) * HD] = at[:, j * T : (j + 1) * T].T
-    a_c = go(rcopy(att_t.at[:, other], lhs.at[1], core_ss.at[1], core_rs.at[1], mate))
+        heads = pl.ds(g * 16, 16)
+        to_mate = rcopy(
+            att_t.at[heads, other], lhs.at[1, heads], core_ss.at[1 + g], core_rs.at[1 + g], mate
+        )
+        a_c.append(go(to_mate))
     loc[4].wait()
     for i, s in enumerate(D7):
         there = w_full.at[(z - s + 8) % 8, xl, k]
@@ -184,7 +190,8 @@
     dy_c.wait_recv()
     order_columns(1)
     lhs[0] = att_t[:, k]
-    a_c.wait_recv()
+    for cp in a_c:
+        cp.wait_recv()
     left = jnp.concatenate([lhs[0], lhs[1]], axis=2).reshape(8, 4, 16, 2 * T)
     g_a = jnp.dot(left[:, :2].reshape(256, 2 * T), dyp[...], preferred_element_type=F32)
     ga[...] = g_a.astype(BF).reshape(8, 2, 16, D)
@@ -341,7 +348,7 @@
         dma((7,)), dma((7,)),
         dma((6,)), dma((6,)),
         dma((7,)), dma((1,)),
-        dma((2,)), dma((2,)),
+        dma((3,)), dma((3,)),
         dma((4,)), dma((4,)),
         dma((7,)), dma((7,)),
         dma((7,)), dma((7,)),

time: 61.6 us -> 62.4 us (1.013)
  Pallas kernels: 60.8 us -> 61.6 us
    pallas_call x1, Pallas kernels: 60 us -> 60.8 us  [shards(): pl.pallas_call(kernel, out_shape=(vm((T, D), BF), vm((T, D), BF), vm((T,...]
where the time goes in v6:
time: 62.4 us; the launch traced here: 62.3 us
  Pallas kernels  61.6 us (99%)
  between operations  0.64 us (1%)
    pallas_call x1, Pallas kernels, shards(): pl.pallas_call(kernel, out_shape=(vm((T, D), BF), vm((T, D), BF), vm((T,...  60.8 us

profile of v6, /device:TPU:1, one launch (start us, length us, event | category | flops | bytes accessed | tf_op | source)
XLA Modules:
  0.0 62.3 jit_solution(17942346222866848838)
XLA Ops:
  0.6 60.8 %sublayer.1 = (bf16[128,1024]{1,0:T(8,128)(2,1)S(1)}, bf16[128,1024]{1,0:T(8,128)(2,1)S(1)}, bf16[128,256]{1,0:T(8,128)(2,1)S(1)}, bf16[128,256]{1,0:T(8,128)(2,1)S(1)}, f32[16,64]{1,0:T(8,128)S(1)}) custom-call(s32[1,128]{1,0:T(1,128)} %bitcast.19, s32[4,8]{1,0:T(4,128)} %bitcast.18, bf16[128,1024]{1,0:T(8,128)(2,1)} %bitcast.10, ...), custom_call_target="tpu_custom_call" | custom-call | flops 1400000000 | bytes 1500000 | tf_op jit(solution)/shard_map/sublayer/pallas_call | solution.py:359
  61.4 0.9 %store.1 = (bf16[128,1024]{1,0:T(8,128)(2,1)}, bf16[128,1024]{1,0:T(8,128)(2,1)}, bf16[128,256]{1,0:T(8,128)(2,1)}, bf16[128,256]{1,0:T(8,128)(2,1)}, f32[16,64]{1,0:T(8,128)}) custom-call(bf16[128,1024]{1,0:T(8,128)(2,1)S(1)} %get-tuple-element.15.refs_0_, bf16[128,1024]{1,0:T(8,128)(2,1)S(1)} %get-tuple-element.16.refs_1_, ...), custom_call_target="tpu_custom_call" | custom-call | tf_op jit(solution)/shard_map/store/pallas_call | solution.py:381
